TPU v7x, 32 devices: a whole 2x2x4 slice. The times are simulated.
32 devices in a mesh: groups: 2 (over y), dp: 4 (over x, core), tensor: 4 (over z).
Axes of the slice: x: 2, y: 2, z: 4, core: 2. Of those that a mesh axis runs over, the one named last changes fastest.
Arguments:
- gate_pre: bfloat16 [4096, 13824], P(('groups', 'dp'), 'tensor'), parts along dimension 0, may hold values from -6 to 6
- up_pre: bfloat16 [4096, 13824], P(('groups', 'dp'), 'tensor'), parts along dimension 0, may hold values from -6 to 6
- d_out: bfloat16 [4096, 5120], P(('groups', 'dp'), 'tensor'), parts along dimension 0, may hold values from -6 to 6
- lengths: int32 [32], P(('groups', 'dp')), parts along dimension 0, may hold values from 1 to 128, 1280 in all
- w_gate: bfloat16 [5120, 13824], P('dp', 'tensor'), may hold values from -0.0546875 to 0.0546875
- w_up: bfloat16 [5120, 13824], P('dp', 'tensor'), may hold values from -0.0546875 to 0.0546875
- w_down: bfloat16 [13824, 5120], P('tensor', 'dp'), may hold values from -0.078125 to 0.078125
- buckets_ff: int32 [13824], P('tensor'), may hold values from 0 to 255
- signs_ff: int32 [13824], P('tensor'), may hold values from 0 to 1
- buckets_d: int32 [5120], replicated, may hold values from 0 to 255
- signs_d: int32 [5120], replicated, may hold values from 0 to 1
- queries: bfloat16 [4096, 65536], P('dp', 'tensor'), may hold values from -6 to 6
Outputs:
- grad_input: bfloat16 [4096, 5120], P(('groups', 'dp'), 'tensor'), parts along dimension 0
- scores: float32 [8192, 16], P(('groups', 'dp')), parts along dimension 0
There are 2 independent parts, one for each index of `groups`. A program takes and returns all parts, laid end to end along the dimension named above; an argument that names none is the same for every part. Nothing has to cross between parts.
Inputs may be any that keep to these rules, and one draw needn't show every extreme that they name: The 4 lengths of each index of dp sum to at most 512; in each part along groups all lengths sum to 1280; the largest in each part is exactly 128.
All inputs are finite; a program needn't handle non-finite values.
Results may differ from a plain program's by a relative error of at most 0.0095.
Values may be sent and summed in bfloat16 or wider, within the bound.
A program may use at most 384 MiB of HBM per device.

v0:
```python
import jax
import jax.numpy as jnp
from jax import lax
from jax.sharding import PartitionSpec as P

SK = 256


def sign_table(buckets, signs):
    hits = buckets[:, None] == jnp.arange(SK, dtype=jnp.int32)[None, :]
    values = (2 * signs - 1).astype(jnp.float32)[:, None]
    return jnp.where(hits, values, jnp.float32(0.0)).astype(jnp.bfloat16)


def contract_last(left, right):
    return lax.dot_general(
        left, right, (((1,), (1,)), ((), ())), preferred_element_type=jnp.float32
    )


def example_pairs(left, right, member, starts, span):
    results = []
    for example in range(member.shape[1]):
        rows_left = lax.dynamic_slice_in_dim(left, starts[example], span, 0)
        rows_right = lax.dynamic_slice_in_dim(right, starts[example], span, 0)
        inside = lax.dynamic_slice_in_dim(member[:, example], starts[example], span, 0)
        results.append(
            lax.dot_general(
                rows_left * inside[:, None],
                rows_right,
                (((0,), (0,)), ((), ())),
                precision=lax.Precision.HIGHEST,
                preferred_element_type=jnp.float32,
            )
        )
    return jnp.stack(results, axis=0)


def local(
    gate_pre,
    up_pre,
    d_out,
    lengths,
    w_gate,
    w_up,
    w_down,
    buckets_ff,
    signs_ff,
    buckets_d,
    signs_d,
    queries,
):
    tok_count = gate_pre.shape[0]
    ex_count = lengths.shape[0]
    finish = jnp.cumsum(lengths)
    starts = finish - lengths
    row_ids = jnp.arange(tok_count, dtype=jnp.int32)[:, None]
    member = ((row_ids >= starts[None, :]) & (row_ids < finish[None, :])).astype(jnp.float32)
    live_rows = jnp.sum(member, axis=1)
    d_full = lax.all_gather(d_out, "tensor", axis=1, tiled=True)
    d_live = jnp.where(live_rows[:, None] > 0, d_full, jnp.zeros_like(d_full))
    grad_hidden = contract_last(d_live, lax.all_gather(w_down, "dp", axis=1, tiled=True))
    gate_val = gate_pre.astype(jnp.float32)
    up_val = up_pre.astype(jnp.float32)
    sigmoid_gate = jax.nn.sigmoid(gate_val)
    silu_gate = gate_val * sigmoid_gate
    hidden = (silu_gate * up_val).astype(jnp.bfloat16)
    grad_gate = (
        grad_hidden * up_val * sigmoid_gate * (1.0 + gate_val * (1.0 - sigmoid_gate))
    ).astype(jnp.bfloat16)
    grad_up = (grad_hidden * silu_gate).astype(jnp.bfloat16)
    part_cols = contract_last(
        grad_gate, lax.all_gather(w_gate, "dp", axis=0, tiled=True)
    ) + contract_last(grad_up, lax.all_gather(w_up, "dp", axis=0, tiled=True))
    partial_low = part_cols.astype(jnp.bfloat16)
    grad_input = (
        lax.psum_scatter(partial_low, "tensor", scatter_dimension=1, tiled=True)
        .astype(jnp.float32)
        .astype(jnp.bfloat16)
    )
    table_ff = sign_table(buckets_ff, signs_ff)
    table_model = sign_table(buckets_d, signs_d)
    hidden_sketch = jnp.dot(hidden, table_ff, preferred_element_type=jnp.float32)
    grad_sketch = jnp.dot(d_live, table_model, preferred_element_type=jnp.float32)
    bucket_rows = SK // lax.axis_size("tensor")
    span = tok_count // 4
    summed_sketch = lax.psum_scatter(hidden_sketch, "tensor", scatter_dimension=1, tiled=True)
    sketch = example_pairs(summed_sketch, grad_sketch, member, starts, span)
    sketch = sketch.reshape(ex_count, bucket_rows * SK)
    sketch_low = sketch.astype(jnp.bfloat16)
    all_sketches = lax.all_gather(sketch_low, "dp", axis=0, tiled=True)
    raw_scores = contract_last(queries, all_sketches)
    sketch_val = all_sketches.astype(jnp.float32)
    squares = jnp.sum(sketch_val * sketch_val, axis=1)
    raw_scores, squares = lax.psum((raw_scores, squares), "tensor")
    scores = raw_scores * lax.rsqrt(squares + 1e-06)[None, :]
    return (grad_input, scores)


def solution(mesh):
    in_specs = (
        P(("groups", "dp"), "tensor"),
        P(("groups", "dp"), "tensor"),
        P(("groups", "dp"), "tensor"),
        P(("groups", "dp")),
        P("dp", "tensor"),
        P("dp", "tensor"),
        P("tensor", "dp"),
        P("tensor"),
        P("tensor"),
        P(),
        P(),
        P("dp", "tensor"),
    )
    out_specs = (P(("groups", "dp"), "tensor"), P(("groups", "dp"), None))
    return jax.shard_map(local, mesh=mesh, in_specs=in_specs, out_specs=out_specs, check_vma=False)
```

profile of v0, /device:TPU:0, one launch (start us, length us, event | category | flops | bytes accessed | tf_op | source)
XLA Modules:
  0.0 918.6 jit_solution(10579860210606448549)
XLA Ops:
  7.2 0.7 all-gather.6.cloned.1.call-update
  7.9 0.7 add_convert_fusion.2
  8.7 7.4 fusion.8
  16.1 0.7 all-gather.8.cloned.1.call-update
  17.5 0.5 all-gather.12.cloned.1.call-update
  18.3 0.6 fusion.60
  26.6 83.8 %all-gather.6.cloned.1.call-done = bf16[512,5120]{1,0:T(8,128)(2,1)} async-done(((bf16[512,1280]{1,0:T(8,128)(2,1)}), bf16[512,5120]{1,0:T(8,128)(2,1)}) %all-gather.6.cloned.1.call-update) | async-done | bytes 5242896 | tf_op jit(solution)/shard_map/all_gather | solution.py:60
  110.4 4.3 fusion.13
  114.7 18.6 %reduce-scatter.5.cloned.1.call-done = f32[512,64]{0,1:T(8,128)} async-done(((f32[512,256]{0,1:T(8,128)}), f32[512,64]{0,1:T(8,128)}) %reduce-scatter.5.cloned.1.call-update) | async-done | bytes 131088 | tf_op jit(solution)/shard_map/reduce_scatter | solution.py:87
  133.2 1.1 fusion.21
  134.4 1.1 fusion.22
  135.5 1.1 fusion.23
  136.7 1.1 fusion.24
  138.2 7.1 all-gather
  145.5 22.0 %convolution_bitcast_fusion = f32[1024,16]{0,1:T(8,128)} fusion(bf16[16,16384]{1,0:T(8,128)(2,1)S(1)} %reshape.61, bf16[1024,16384]{1,0:T(8,128)(2,1)} %param.23), kind=kOutput, calls=%fused_computation.31 | convolution fusion | flops 536870912 | bytes 34144256 | tf_op jit(solution)/shard_map/dot_general | solution.py:16
  167.7 179.6 %all-gather.8.cloned.1.call-done = bf16[3456,5120]{1,0:T(8,128)(2,1)} async-done(((bf16[3456,1280]{1,0:T(8,128)(2,1)}), bf16[3456,5120]{1,0:T(8,128)(2,1)}) %all-gather.8.cloned.1.call-update) | async-done | bytes 35389456 | tf_op jit(solution)/shard_map/all_gather | solution.py:62
  347.3 29.0 %fusion.17 = f32[512,3456]{1,0:T(8,128)} fusion(bf16[3456,5120]{1,0:T(8,128)(2,1)} %all-gather.8.cloned.1.call-done, bf16[512,5120]{1,0:T(8,128)(2,1)} %all-gather.6.cloned.1.call-done, pred[512]{0:T(512)(128)(4,1)S(1)} %broadcast_compare_fusion), kind=kOutput, calls=%fused_computation.27 | convolution fusion | flops 18122014720 | bytes 47710720 | tf_op jit(solution)/shard_map/dot_general | solution.py:16
  376.2 186.7 %all-gather.10.cloned.1.call-done = bf16[5120,3456]{1,0:T(8,128)(2,1)} async-done(((bf16[1280,3456]{1,0:T(8,128)(2,1)}), bf16[5120,3456]{1,0:T(8,128)(2,1)}) %all-gather.10.cloned.1.call-update) | async-done | bytes 35389456 | tf_op jit(solution)/shard_map/all_gather | solution.py:73
  562.9 37.5 %fusion.10 = f32[512,5120]{1,0:T(8,128)} fusion(bf16[5120,3456]{1,0:T(8,128)(2,1)} %all-gather.10.cloned.1.call-done, f32[512,3456]{1,0:T(8,128)} %fusion.17, bf16[512,3456]{1,0:T(8,128)(2,1)} %param.13, bf16[512,3456]{1,0:T(8,128)(2,1)} %param.12), kind=kOutput, calls=%fused_computation.19 | convolution fusion | flops 18140626944 | bytes 60030976 | tf_op jit(solution)/shard_map/dot_general | solution.py:16
  600.4 178.1 %all-gather.12.cloned.1.call-done = bf16[5120,3456]{1,0:T(8,128)(2,1)} async-done(((bf16[1280,3456]{1,0:T(8,128)(2,1)}), bf16[5120,3456]{1,0:T(8,128)(2,1)}) %all-gather.12.cloned.1.call-update) | async-done | bytes 35389456 | tf_op jit(solution)/shard_map/all_gather | solution.py:74
  778.5 32.3 %add_convert_fusion = bf16[512,5120]{1,0:T(8,128)(2,1)} fusion(f32[512,5120]{1,0:T(8,128)} %fusion.10, bf16[5120,3456]{1,0:T(8,128)(2,1)} %all-gather.12.cloned.1.call-done, f32[512,3456]{1,0:T(8,128)} %fusion.17, bf16[512,3456]{1,0:T(8,128)(2,1)} %param.12), kind=kOutput, calls=%fused_computation.3 | convolution fusion | flops 18137022464 | bytes 61734912 | tf_op jit(solution)/shard_map/dot_general | solution.py:16
  811.1 11.7 %psum.15 = f32[16]{0:T(128)S(1)} all-reduce(f32[16]{0:T(128)S(1)} %multiply_reduce_fusion), channel_id=1, replica_groups=mesh['groups'=2,'dp'=4,'tensor'=4] {'tensor'}, use_global_device_ids=true, to_apply=%region_6.7 | all-reduce | flops 16 | bytes 128 | tf_op jit(solution)/shard_map/psum | solution.py:95
  822.8 1.6 broadcast_multiply_fusion
  824.4 87.3 %reduce-scatter.3.cloned.1.call-done = bf16[512,1280]{1,0:T(8,128)(2,1)} async-done(((bf16[512,5120]{1,0:T(8,128)(2,1)}), bf16[512,1280]{1,0:T(8,128)(2,1)}) %reduce-scatter.3.cloned.1.call-update) | async-done | bytes 1310736 | tf_op jit(solution)/shard_map/reduce_scatter | solution.py:77
  (35 shorter events, 2.5 us)
Async XLA Ops:
  7.2 103.2 %all-gather.6.cloned.1.call-start = ((), (), s32[]{:S(2)}) async-start(), calls=%async_computation.2 | async-start | bytes 6553600 | tf_op jit(solution)/shard_map/all_gather | solution.py:60
  7.9 125.3 %reduce-scatter.5.cloned.1.call-start = ((), (), s32[]{:S(2)}) async-start(), calls=%async_computation.7 | async-start | bytes 655360 | tf_op jit(solution)/shard_map/reduce_scatter | solution.py:87
  16.1 331.2 %all-gather.8.cloned.1.call-start = ((), (), s32[]{:S(2)}) async-start(), calls=%async_computation.3 | async-start | bytes 44236800 | tf_op jit(solution)/shard_map/all_gather | solution.py:62
  16.8 1.2 copy-start.2
  16.8 9.7 %copy-start = (s32[5120]{0:T(1024)S(1)}, s32[5120]{0:T(1024)}, u32[]{:S(2)}) copy-start(s32[5120]{0:T(1024)} %param.22) | copy-start | bytes 61444
  16.8 93.5 %copy-start.1 = (s32[5120]{0:T(1024)S(1)}, s32[5120]{0:T(1024)}, u32[]{:S(2)}) copy-start(s32[5120]{0:T(1024)} %param.21) | copy-start | bytes 61444
  16.8 546.0 %all-gather.10.cloned.1.call-start = ((), (), s32[]{:S(2)}) async-start(), calls=%async_computation.4 | async-start | bytes 44236800 | tf_op jit(solution)/shard_map/all_gather | solution.py:73
  17.4 761.1 %all-gather.12.cloned.1.call-start = ((), (), s32[]{:S(2)}) async-start(), calls=%async_computation.5 | async-start | bytes 44236800 | tf_op jit(solution)/shard_map/all_gather | solution.py:74
  18.0 804.8 %all-reduce.2.cloned.1.call-start = ((), (), s32[]{:S(2)}) async-start(), calls=%async_computation.8 | async-start | bytes 131072 | tf_op jit(solution)/shard_map/psum | solution.py:95
  167.5 744.3 %reduce-scatter.3.cloned.1.call-start = ((), (), s32[]{:S(2)}) async-start(), calls=%async_computation.6 | async-start | bytes 6553600 | tf_op jit(solution)/shard_map/reduce_scatter | solution.py:77
Sparse Core Ops, SparseCore 0:
  9.6 100.7 all-gather.5
  113.2 19.9 reduce-scatter.4
  134.8 212.4 all-gather.7
  348.7 214.1 all-gather.9
  564.3 214.1 all-gather.11
  781.3 33.9 all-reduce.1
  818.3 93.4 reduce-scatter.2
where the time goes:
time: 919 us
  waiting for transfers between devices  737 us (80%)
  matrix products  137 us (15%)
  between operations  21.6 us (2%)
  blocking collectives  18.8 us (2%)
    all_gather x1, waiting for transfers between devices, local(): lax.all_gather(w_gate, 'dp', axis=0, tiled=True)  187 us
    all_gather x1, waiting for transfers between devices, local(): lax.all_gather(w_down, 'dp', axis=1, tiled=True)  180 us
    all_gather x1, waiting for transfers between devices, local(): lax.all_gather(w_up, 'dp', axis=0, tiled=True)  178 us
    dot_general x4, matrix products, contract_last(): lax.dot_general(left, right, (((1,), (1,)), ((), ())), preferred_element_...  121 us
    reduce_scatter x1, waiting for transfers between devices, local(): lax.psum_scatter(partial_low, 'tensor', scatter_dimension=1, tiled=True)  87.3 us
    all_gather x1, waiting for transfers between devices, local(): d_full = lax.all_gather(d_out, 'tensor', axis=1, tiled=True)  83.8 us
    reduce_scatter x1, waiting for transfers between devices, local(): lax.psum_scatter(hidden_sketch, 'tensor', scatter_dimension=1, tiled=True)  18.6 us
  transfers between devices with their start and end apart: 7, of which 6 were waited for; matrix products, arithmetic and copies ran while one was open for 15% of the time, Pallas kernels for 0%

commit v1 on v0

--- a/solution.py
+++ b/solution.py
@@ -34,6 +34,61 @@
             )
         )
     return jnp.stack(results, axis=0)
+
+
+def swap_dp(value, bit):
+    count = lax.axis_size("dp")
+    return lax.ppermute(value, "dp", [(k, k ^ bit) for k in range(count)])
+
+
+def swap_groups(value):
+    return lax.ppermute(value, "groups", [(0, 1), (1, 0)])
+
+
+def after(value, earlier):
+    return lax.optimization_barrier((value, *earlier))[0]
+
+
+def spread(blocks, done):
+    group = lax.axis_index("groups")
+    half = blocks[0].shape[1] // 2
+    sides, nears, others = [], [], []
+    for block in blocks:
+        mine = lax.dynamic_slice_in_dim(block, group * half, half, 1)
+        nears.append(swap_dp(after(mine, done[2]), 2))
+    for block in blocks:
+        sides.append(swap_dp(after(block, done[1]), 1))
+    nears = [after(near, done[1]) for near in nears]
+    others = [after(swap_groups(near), done[0]) for near in nears]
+
+    def join(first, second):
+        low = jnp.where(group == 0, first, second)
+        high = jnp.where(group == 0, second, first)
+        return jnp.concatenate([low, high], axis=1)
+
+    results = []
+    for block, side, near, other in zip(blocks, sides, nears, others):
+        far = join(near, other)
+        far_side = join(swap_dp(near, 1), swap_dp(other, 1))
+        results.append([block, side, far, far_side])
+    return results
+
+
+def in_order(parts):
+    k = lax.axis_index("dp")
+    odd, far = (k % 2) == 1, k >= 2
+    a, b, c, d = parts
+    a, b = jnp.where(odd, b, a), jnp.where(odd, a, b)
+    c, d = jnp.where(odd, d, c), jnp.where(odd, c, d)
+    return [
+        jnp.where(far, c, a),
+        jnp.where(far, d, b),
+        jnp.where(far, a, c),
+        jnp.where(far, b, d),
+    ]
+
+DOWN_PIECES = 4
+UP_TENTHS = (2, 2, 2, 2, 1, 1)
 
 
 def local(
@@ -59,7 +114,22 @@
     live_rows = jnp.sum(member, axis=1)
     d_full = lax.all_gather(d_out, "tensor", axis=1, tiled=True)
     d_live = jnp.where(live_rows[:, None] > 0, d_full, jnp.zeros_like(d_full))
-    grad_hidden = contract_last(d_live, lax.all_gather(w_down, "dp", axis=1, tiled=True))
+    columns = w_down.shape[1]
+    k = lax.axis_index("dp")
+    d_blocks = [
+        lax.dynamic_slice_in_dim(d_live, (k ^ r) * columns, columns, 1) for r in range(4)
+    ]
+    pieces = []
+    done = [(), (), ()]
+    rows = w_down.shape[0] // DOWN_PIECES
+    for p in range(DOWN_PIECES):
+        (blocks,) = spread([w_down[None, p * rows : (p + 1) * rows]], done)
+        total = contract_last(d_blocks[0], blocks[0][0])
+        for r in range(1, 4):
+            total = total + contract_last(d_blocks[r], blocks[r][0])
+        pieces.append(total)
+        done = [(total,)] + done[:2]
+    grad_hidden = jnp.concatenate(pieces, axis=1)
     gate_val = gate_pre.astype(jnp.float32)
     up_val = up_pre.astype(jnp.float32)
     sigmoid_gate = jax.nn.sigmoid(gate_val)
@@ -69,15 +139,6 @@
         grad_hidden * up_val * sigmoid_gate * (1.0 + gate_val * (1.0 - sigmoid_gate))
     ).astype(jnp.bfloat16)
     grad_up = (grad_hidden * silu_gate).astype(jnp.bfloat16)
-    part_cols = contract_last(
-        grad_gate, lax.all_gather(w_gate, "dp", axis=0, tiled=True)
-    ) + contract_last(grad_up, lax.all_gather(w_up, "dp", axis=0, tiled=True))
-    partial_low = part_cols.astype(jnp.bfloat16)
-    grad_input = (
-        lax.psum_scatter(partial_low, "tensor", scatter_dimension=1, tiled=True)
-        .astype(jnp.float32)
-        .astype(jnp.bfloat16)
-    )
     table_ff = sign_table(buckets_ff, signs_ff)
     table_model = sign_table(buckets_d, signs_d)
     hidden_sketch = jnp.dot(hidden, table_ff, preferred_element_type=jnp.float32)
@@ -94,6 +155,30 @@
     squares = jnp.sum(sketch_val * sketch_val, axis=1)
     raw_scores, squares = lax.psum((raw_scores, squares), "tensor")
     scores = raw_scores * lax.rsqrt(squares + 1e-06)[None, :]
+    width = d_out.shape[1]
+    outer = w_gate.shape[0] // width
+    gate_rows = w_gate.reshape(outer, width, w_gate.shape[1])
+    up_rows = w_up.reshape(outer, width, w_up.shape[1])
+    finals = []
+    begin = 0
+    for p, tenths in enumerate(UP_TENTHS):
+        step = width * tenths // 10
+        picked = slice(begin, begin + step)
+        begin += step
+        gate_blocks, up_blocks = spread([gate_rows[:, picked], up_rows[:, picked]], done)
+        parts = []
+        for gate_block, up_block in zip(gate_blocks, up_blocks):
+            flat = (outer * step, w_gate.shape[1])
+            parts.append(
+                (
+                    contract_last(grad_gate, gate_block.reshape(flat))
+                    + contract_last(grad_up, up_block.reshape(flat))
+                ).astype(jnp.bfloat16)
+            )
+        part = jnp.concatenate(in_order(parts), axis=1)
+        finals.append(lax.psum_scatter(part, "tensor", scatter_dimension=1, tiled=True))
+        done = [(part,) if p != 1 else (part, scores)] + done[:2]
+    grad_input = jnp.concatenate(finals, axis=1)
     return (grad_input, scores)
 
 

time: 919 us -> 627 us (0.68)
  waiting for transfers between devices: 737 us -> 250 us
  local copies, waits for them, and re-layouts: 1.14 us -> 70.7 us
  other arithmetic: 3.21 us -> 62.5 us
  starting transfers between devices: 0.45 us -> 42.3 us
  matrix products: 137 us -> 151 us
    all_gather x3 -> x0, waiting for transfers between devices: 544 us -> none  [the longest x1 187 us: local(): lax.all_gather(w_gate, 'dp', axis=0, tiled=True)]
    ppermute x0 -> x80, waiting for transfers between devices: none -> 235 us  [the longest x16 129 us: swap_groups(): return lax.ppermute(value, 'groups', [(0, 1), (1, 0)])]
    all_gather x1, waiting for transfers between devices: 83.8 us -> 0.02 us  [local(): d_full = lax.all_gather(d_out, 'tensor', axis=1, tiled=True)]
    reduce_scatter x1 -> x6, waiting for transfers between devices: 87.3 us -> 14.2 us  [local(): lax.psum_scatter(part, 'tensor', scatter_dimension=1, tiled=True)]
    select_n x0 -> x33, other arithmetic: none -> 48 us  [the longest x32 45.1 us: join(): low = jnp.where(group == 0, first, second)]
    ppermute x0 -> x80, starting transfers between devices: none -> 41 us  [the longest x64 22.6 us: swap_dp(): return lax.ppermute(value, 'dp', [(k, k ^ bit) for k in range(count)])]
    unnamed x11 -> x121, local copies, waits for them, and re-layouts: 0.35 us -> 23.4 us
    reduce_scatter x1, waiting for transfers between devices: 18.6 us -> 0.02 us  [local(): lax.psum_scatter(hidden_sketch, 'tensor', scatter_dimension=1, tiled=True)]
  transfers between devices with their start and end apart: 7 -> 89, of which waited for: 6 -> 24; matrix products, arithmetic and copies ran while one was open for 15% -> 44% of each run, Pallas kernels for 0% -> 0%
where the time goes in v1:
time: 627 us; the launch traced here: 620 us
  waiting for transfers between devices  250 us (40%)
  matrix products  151 us (24%)
  local copies, waits for them, and re-layouts  70.7 us (11%)
  other arithmetic  62.5 us (10%)
  starting transfers between devices  42.3 us (7%)
  between operations  23.7 us (4%)
  blocking collectives  19.8 us (3%)
    dot_general x65, matrix products, contract_last(): lax.dot_general(left, right, (((1,), (1,)), ((), ())), preferred_element_...  139 us
    ppermute x16, waiting for transfers between devices, swap_groups(): return lax.ppermute(value, 'groups', [(0, 1), (1, 0)])  129 us
    ppermute x64, waiting for transfers between devices, swap_dp(): return lax.ppermute(value, 'dp', [(k, k ^ bit) for k in range(count)])  105 us
    select_n x32, other arithmetic, join(): low = jnp.where(group == 0, first, second)  45.1 us
    unnamed x121, local copies, waits for them, and re-layouts  23.4 us
    ppermute x64, starting transfers between devices, swap_dp(): return lax.ppermute(value, 'dp', [(k, k ^ bit) for k in range(count)])  22.6 us
    ppermute x16, starting transfers between devices, swap_groups(): return lax.ppermute(value, 'groups', [(0, 1), (1, 0)])  18.4 us
    dynamic_slice x10, local copies, waits for them, and re-layouts, spread(): mine = lax.dynamic_slice_in_dim(block, group * half, half, 1)  18.2 us
  transfers between devices with their start and end apart: 89, of which 24 were waited for; matrix products, arithmetic and copies ran while one was open for 44% of the time, Pallas kernels for 0%

profile of v1, /device:TPU:0, one launch (start us, length us, event | category | flops | bytes accessed | tf_op | source)
XLA Modules:
  0.0 620.1 jit_solution(9721909997169064850)
XLA Ops:
  8.0 7.1 %slice_bitcast_fusion = (bf16[1,864,1280]{2,1,0:T(8,128)(2,1)}, bf16[1,864,1280]{2,1,0:T(8,128)(2,1)}, bf16[1,864,1280]{2,1,0:T(8,128)(2,1)}, bf16[1,864,1280]{2...) fusion(bf16[3456,1280]{1,0:T(8,128)(2,1)} %param.18), kind=kLoop, calls=%fused_computation.529 | loop fusion | bytes 26542080 | tf_op jit(solution)/shard_map/broadcast_in_dim | solution.py:126
  25.2 6.2 copy.18
  31.4 6.4 %fusion.8 = f32[512,256]{0,1:T(8,128)} fusion(bf16[512,3456]{0,1:T(8,128)(2,1)S(1)} %copy.17, bf16[512,3456]{0,1:T(8,128)(2,1)} %copy.18, bf16[3456]{0:T(1024)(128)(2,1)S(1)} %add_convert_fusion.1, s32[3456]{0:T(1024)} %param.19), kind=kOutput, calls=%fused_computation.18 | convolution fusion | flops 921894912 | bytes 7622912 | tf_op jit(solution)/shard_map/dot_general | solution.py:144
  47.5 5.7 fusion.357
  83.6 16.2 %collective-permute-done.2 = bf16[1,432,1280]{2,1,0:T(8,128)(2,1)} collective-permute-done((bf16[1,432,1280]{2,1,0:T(8,128)(2,1)}, bf16[1,432,1280]{2,1,0:T(8,128)(2,1)}, u32[]{:S(2)}, u32[]{:S(2)}) %collective-permute-start.2) | collective-permute-done | bytes 1105952 | tf_op jit(solution)/shard_map/ppermute | solution.py:45
  141.7 7.4 %all-gather = bf16[4,4,16384]{2,1,0:T(4,128)(2,1)S(1)} all-gather(bf16[1,4,16384]{2,1,0:T(4,128)(2,1)S(1)} %maximum_bitcast_fusion.104), channel_id=1, replica_groups=mesh['groups'=2,'dp'=4,'tensor'=4] {'dp'}, dimensions={0}, use_global_device_ids=true | all-gather | bytes 655360 | tf_op jit(solution)/shard_map/all_gather | solution.py:152
  149.3 15.1 %convolution_bitcast_fusion = f32[1024,16]{0,1:T(8,128)} fusion(bf16[16,16384]{1,0:T(8,128)(2,1)S(1)} %reshape.265, bf16[1024,16384]{1,0:T(8,128)(2,1)} %param.23), kind=kOutput, calls=%fused_computation.216 | convolution fusion | flops 536870912 | bytes 34144256 | tf_op jit(solution)/shard_map/dot_general | solution.py:16
  175.0 12.3 %psum.15 = f32[16]{0:T(128)S(1)} all-reduce(f32[16]{0:T(128)S(1)} %multiply_reduce_fusion), channel_id=1, replica_groups=mesh['groups'=2,'dp'=4,'tensor'=4] {'tensor'}, use_global_device_ids=true, to_apply=%region_7.8 | all-reduce | flops 16 | bytes 128 | tf_op jit(solution)/shard_map/psum | solution.py:156
  206.8 14.8 %collective-permute-done.16 = bf16[1,432,1280]{2,1,0:T(8,128)(2,1)} collective-permute-done((bf16[1,432,1280]{2,1,0:T(8,128)(2,1)}, bf16[1,432,1280]{2,1,0:T(8,128)(2,1)}, u32[]{:S(2)}, u32[]{:S(2)}) %collective-permute-start.16) | collective-permute-done | bytes 1105952 | tf_op jit(solution)/shard_map/ppermute | solution.py:41
  236.2 14.1 %collective-permute-done.24 = bf16[1,128,3456]{2,1,0:T(8,128)(2,1)} collective-permute-done((bf16[1,128,3456]{2,1,0:T(8,128)(2,1)S(1)}, bf16[1,128,3456]{2,1,0:T(8,128)(2,1)}, u32[]{:S(2)}, u32[]{:S(2)}) %collective-permute-start.24) | collective-permute-done | bytes 884768 | tf_op jit(solution)/shard_map/ppermute | solution.py:41
  250.9 18.1 %collective-permute-done.20 = bf16[1,128,3456]{2,1,0:T(8,128)(2,1)} collective-permute-done((bf16[1,128,3456]{2,1,0:T(8,128)(2,1)S(1)}, bf16[1,128,3456]{2,1,0:T(8,128)(2,1)}, u32[]{:S(2)}, u32[]{:S(2)}) %collective-permute-start.20) | collective-permute-done | bytes 884768 | tf_op jit(solution)/shard_map/ppermute | solution.py:41
  321.6 15.8 %collective-permute-done.30 = bf16[1,128,3456]{2,1,0:T(8,128)(2,1)} collective-permute-done((bf16[1,128,3456]{2,1,0:T(8,128)(2,1)S(1)}, bf16[1,128,3456]{2,1,0:T(8,128)(2,1)}, u32[]{:S(2)}, u32[]{:S(2)}) %collective-permute-start.30) | collective-permute-done | bytes 884768 | tf_op jit(solution)/shard_map/ppermute | solution.py:41
  351.0 12.3 %collective-permute-done.36 = bf16[1,128,3456]{2,1,0:T(8,128)(2,1)} collective-permute-done((bf16[1,128,3456]{2,1,0:T(8,128)(2,1)}, bf16[1,128,3456]{2,1,0:T(8,128)(2,1)}, u32[]{:S(2)}, u32[]{:S(2)}) %collective-permute-start.36) | collective-permute-done | bytes 884768 | tf_op jit(solution)/shard_map/ppermute | solution.py:45
  365.6 15.8 %collective-permute-done.32 = bf16[1,128,3456]{2,1,0:T(8,128)(2,1)} collective-permute-done((bf16[1,128,3456]{2,1,0:T(8,128)(2,1)}, bf16[1,128,3456]{2,1,0:T(8,128)(2,1)}, u32[]{:S(2)}, u32[]{:S(2)}) %collective-permute-start.32) | collective-permute-done | bytes 884768 | tf_op jit(solution)/shard_map/ppermute | solution.py:45
  385.9 16.5 %collective-permute-done.40 = bf16[1,128,3456]{2,1,0:T(8,128)(2,1)} collective-permute-done((bf16[1,128,3456]{2,1,0:T(8,128)(2,1)S(1)}, bf16[1,128,3456]{2,1,0:T(8,128)(2,1)}, u32[]{:S(2)}, u32[]{:S(2)}) %collective-permute-start.40) | collective-permute-done | bytes 884768 | tf_op jit(solution)/shard_map/ppermute | solution.py:41
  416.0 12.4 %collective-permute-done.46 = bf16[1,128,3456]{2,1,0:T(8,128)(2,1)} collective-permute-done((bf16[1,128,3456]{2,1,0:T(8,128)(2,1)}, bf16[1,128,3456]{2,1,0:T(8,128)(2,1)}, u32[]{:S(2)}, u32[]{:S(2)}) %collective-permute-start.46) | collective-permute-done | bytes 884768 | tf_op jit(solution)/shard_map/ppermute | solution.py:45
  429.0 17.4 %collective-permute-done.42 = bf16[1,128,3456]{2,1,0:T(8,128)(2,1)} collective-permute-done((bf16[1,128,3456]{2,1,0:T(8,128)(2,1)}, bf16[1,128,3456]{2,1,0:T(8,128)(2,1)}, u32[]{:S(2)}, u32[]{:S(2)}) %collective-permute-start.42) | collective-permute-done | bytes 884768 | tf_op jit(solution)/shard_map/ppermute | solution.py:45
  470.5 11.1 %collective-permute-done.56 = bf16[1,128,3456]{2,1,0:T(8,128)(2,1)} collective-permute-done((bf16[1,128,3456]{2,1,0:T(8,128)(2,1)}, bf16[1,128,3456]{2,1,0:T(8,128)(2,1)}, u32[]{:S(2)}, u32[]{:S(2)}) %collective-permute-start.56) | collective-permute-done | bytes 884768 | tf_op jit(solution)/shard_map/ppermute | solution.py:45
  483.6 16.1 %collective-permute-done.52 = bf16[1,128,3456]{2,1,0:T(8,128)(2,1)} collective-permute-done((bf16[1,128,3456]{2,1,0:T(8,128)(2,1)}, bf16[1,128,3456]{2,1,0:T(8,128)(2,1)}, u32[]{:S(2)}, u32[]{:S(2)}) %collective-permute-start.52) | collective-permute-done | bytes 884768 | tf_op jit(solution)/shard_map/ppermute | solution.py:45
  504.1 7.1 %collective-permute-done.64 = bf16[1,64,3456]{2,1,0:T(8,128)(2,1)} collective-permute-done((bf16[1,64,3456]{2,1,0:T(8,128)(2,1)S(1)}, bf16[1,64,3456]{2,1,0:T(8,128)(2,1)}, u32[]{:S(2)}, u32[]{:S(2)}) %collective-permute-start.64) | collective-permute-done | bytes 442400 | tf_op jit(solution)/shard_map/ppermute | solution.py:41
  524.5 11.6 %collective-permute-done.62 = bf16[1,64,3456]{2,1,0:T(8,128)(2,1)} collective-permute-done((bf16[1,64,3456]{2,1,0:T(8,128)(2,1)}, bf16[1,64,3456]{2,1,0:T(8,128)(2,1)}, u32[]{:S(2)}, u32[]{:S(2)}) %collective-permute-start.62) | collective-permute-done | bytes 442400 | tf_op jit(solution)/shard_map/ppermute | solution.py:45
  549.6 7.6 %collective-permute-done.74 = bf16[1,64,3456]{2,1,0:T(8,128)(2,1)} collective-permute-done((bf16[1,64,3456]{2,1,0:T(8,128)(2,1)}, bf16[1,64,3456]{2,1,0:T(8,128)(2,1)}, u32[]{:S(2)}, u32[]{:S(2)}) %collective-permute-start.74) | collective-permute-done | bytes 442400 | tf_op jit(solution)/shard_map/ppermute | solution.py:41
  571.8 7.8 %collective-permute-done.72 = bf16[1,64,3456]{2,1,0:T(8,128)(2,1)} collective-permute-done((bf16[1,64,3456]{2,1,0:T(8,128)(2,1)}, bf16[1,64,3456]{2,1,0:T(8,128)(2,1)}, u32[]{:S(2)}, u32[]{:S(2)}) %collective-permute-start.72) | collective-permute-done | bytes 442400 | tf_op jit(solution)/shard_map/ppermute | solution.py:45
  596.7 14.1 %reduce-scatter.20.cloned.1.call-done = bf16[512,128]{0,1:T(8,128)(2,1)} async-done(((bf16[512,512]{0,1:T(8,128)(2,1)}), bf16[512,128]{0,1:T(8,128)(2,1)}) %reduce-scatter.20.cloned.1.call-update) | async-done | bytes 131088 | tf_op jit(solution)/shard_map/reduce_scatter | solution.py:179
  (431 shorter events, 307.4 us)
Async XLA Ops:
  7.2 103.6 %all-gather.3.cloned.1.call-start = ((), (), s32[]{:S(2)}) async-start(), calls=%async_computation.7 | async-start | bytes 6553600 | tf_op jit(solution)/shard_map/all_gather | solution.py:115
  7.9 128.8 %reduce-scatter.12.cloned.1.call-start = ((), (), s32[]{:S(2)}) async-start(), calls=%async_computation.10 | async-start | bytes 655360 | tf_op jit(solution)/shard_map/reduce_scatter | solution.py:148
  16.2 56.6 %collective-permute-start.1 = (bf16[1,432,1280]{2,1,0:T(8,128)(2,1)}, bf16[1,432,1280]{2,1,0:T(8,128)(2,1)}, u32[]{:S(2)}, u32[]{:S(2)}) collective-permute-start(bf16[1,432,1280]{2,1,0:T(8,128)(2,1)} %dynamic-slice_bitcast_fusion.3), channel_id=1, source_target_pairs={{0,8},{4,12},{8,0},{12,4},{1,9},{5,13},{9,1},{13,5},{2,10},{6,14},... | collective-permute-start | bytes 3317768 | tf_op jit(solution)/shard_map/ppermute | solution.py:41
  19.1 100.8 %collective-permute-start = (bf16[1,864,1280]{2,1,0:T(8,128)(2,1)}, bf16[1,864,1280]{2,1,0:T(8,128)(2,1)}, u32[]{:S(2)}, u32[]{:S(2)}) collective-permute-start(bf16[1,864,1280]{2,1,0:T(8,128)(2,1)} %get-tuple-element.133), channel_id=1, source_target_pairs={{0,4},{4,0},{8,12},{12,8},{1,5},{5,1},{9,13},{13,9},{2,6},{6,2},{1... | collective-permute-start | bytes 6635528 | tf_op jit(solution)/shard_map/ppermute | solution.py:41
  20.2 82.3 %collective-permute-start.6 = (bf16[1,432,1280]{2,1,0:T(8,128)(2,1)}, bf16[1,432,1280]{2,1,0:T(8,128)(2,1)}, u32[]{:S(2)}, u32[]{:S(2)}) collective-permute-start(bf16[1,432,1280]{2,1,0:T(8,128)(2,1)} %dynamic-slice_bitcast_fusion.2), channel_id=1, source_target_pairs={{0,8},{4,12},{8,0},{12,4},{1,9},{5,13},{9,1},{13,5},{2,10},{6,14},... | collective-permute-start | bytes 3317768 | tf_op jit(solution)/shard_map/ppermute | solution.py:41
  20.2 176.5 %collective-permute-start.5 = (bf16[1,864,1280]{2,1,0:T(8,128)(2,1)}, bf16[1,864,1280]{2,1,0:T(8,128)(2,1)}, u32[]{:S(2)}, u32[]{:S(2)}) collective-permute-start(bf16[1,864,1280]{2,1,0:T(8,128)(2,1)} %get-tuple-element.134), channel_id=1, source_target_pairs={{0,4},{4,0},{8,12},{12,8},{1,5},{5,1},{9,13},{13,9},{2,6},{6,2},{1... | collective-permute-start | bytes 6635528 | tf_op jit(solution)/shard_map/ppermute | solution.py:41
  37.8 167.4 %all-reduce.2.cloned.1.call-start = ((), (), s32[]{:S(2)}) async-start(), calls=%async_computation.11 | async-start | bytes 131072 | tf_op jit(solution)/shard_map/psum | solution.py:156
  109.0 91.3 %collective-permute-start.8 = (bf16[1,432,1280]{2,1,0:T(8,128)(2,1)}, bf16[1,432,1280]{2,1,0:T(8,128)(2,1)}, u32[]{:S(2)}, u32[]{:S(2)}) collective-permute-start(bf16[1,432,1280]{2,1,0:T(8,128)(2,1)} %collective-permute-done.6), channel_id=1, source_target_pairs={{0,4},{4,0},{8,12},{12,8},{1,5},{5,1},{9,13},{13,9},{2,6},{6,2},{1... | collective-permute-start | bytes 3317768 | tf_op jit(solution)/shard_map/ppermute | solution.py:41
  129.4 75.8 %collective-permute-start.12 = (bf16[1,432,1280]{2,1,0:T(8,128)(2,1)}, bf16[1,432,1280]{2,1,0:T(8,128)(2,1)}, u32[]{:S(2)}, u32[]{:S(2)}) collective-permute-start(bf16[1,432,1280]{2,1,0:T(8,128)(2,1)} %collective-permute-done.11), channel_id=1, source_target_pairs={{0,16},{16,0},{1,17},{17,1},{2,18},{18,2},{3,19},{19,3},{4,20},{20... | collective-permute-start | bytes 3317768 | tf_op jit(solution)/shard_map/ppermute | solution.py:45
  131.2 96.6 %collective-permute-start.13 = (bf16[1,432,1280]{2,1,0:T(8,128)(2,1)}, bf16[1,432,1280]{2,1,0:T(8,128)(2,1)}, u32[]{:S(2)}, u32[]{:S(2)}) collective-permute-start(bf16[1,432,1280]{2,1,0:T(8,128)(2,1)} %collective-permute-done.11), channel_id=1, source_target_pairs={{0,4},{4,0},{8,12},{12,8},{1,5},{5,1},{9,13},{13,9},{2,6},{6,2},{1... | collective-permute-start | bytes 3317768 | tf_op jit(solution)/shard_map/ppermute | solution.py:41
  135.0 65.4 %collective-permute-start.9 = (bf16[1,432,1280]{2,1,0:T(8,128)(2,1)}, bf16[1,432,1280]{2,1,0:T(8,128)(2,1)S(1)}, u32[]{:S(2)}, u32[]{:S(2)}) collective-permute-start(bf16[1,432,1280]{2,1,0:T(8,128)(2,1)} %collective-permute-done.7), channel_id=1, source_target_pairs={{0,4},{4,0},{8,12},{12,8},{1,5},{5,1},{9,13},{13,9},{2,6},{6,2},{1... | collective-permute-start | bytes 3317768 | tf_op jit(solution)/shard_map/ppermute | solution.py:41
  164.4 427.4 %reduce-scatter.8.cloned.1.call-start = ((), (), s32[]{:S(2)}) async-start(), calls=%async_computation.8 | async-start | bytes 1310720 | tf_op jit(solution)/shard_map/reduce_scatter | solution.py:179
  250.9 93.8 %collective-permute-start.25 = (bf16[1,128,3456]{2,1,0:T(8,128)(2,1)}, bf16[1,128,3456]{2,1,0:T(8,128)(2,1)}, u32[]{:S(2)}, u32[]{:S(2)}) collective-permute-start(bf16[1,128,3456]{2,1,0:T(8,128)(2,1)} %collective-permute-done.24), channel_id=1, source_target_pairs={{0,4},{4,0},{8,12},{12,8},{1,5},{5,1},{9,13},{13,9},{2,6},{6,2},{1... | collective-permute-start | bytes 2654216 | tf_op jit(solution)/shard_map/ppermute | solution.py:41
  273.6 63.7 %collective-permute-start.29 = (bf16[1,256,3456]{2,1,0:T(8,128)(2,1)}, bf16[1,256,3456]{2,1,0:T(8,128)(2,1)}, u32[]{:S(2)}, u32[]{:S(2)}) collective-permute-start(bf16[1,256,3456]{2,1,0:T(8,128)(2,1)} %get-tuple-element.73), channel_id=1, source_target_pairs={{0,4},{4,0},{8,12},{12,8},{1,5},{5,1},{9,13},{13,9},{2,6},{6,2},{1... | collective-permute-start | bytes 5308424 | tf_op jit(solution)/shard_map/ppermute | solution.py:41
  273.9 66.6 %collective-permute-start.28 = (bf16[1,256,3456]{2,1,0:T(8,128)(2,1)}, bf16[1,256,3456]{2,1,0:T(8,128)(2,1)}, u32[]{:S(2)}, u32[]{:S(2)}) collective-permute-start(bf16[1,256,3456]{2,1,0:T(8,128)(2,1)} %get-tuple-element.72), channel_id=1, source_target_pairs={{0,4},{4,0},{8,12},{12,8},{1,5},{5,1},{9,13},{13,9},{2,6},{6,2},{1... | collective-permute-start | bytes 5308424 | tf_op jit(solution)/shard_map/ppermute | solution.py:41
  344.7 65.0 %collective-permute-start.35 = (bf16[1,128,3456]{2,1,0:T(8,128)(2,1)}, bf16[1,128,3456]{2,1,0:T(8,128)(2,1)}, u32[]{:S(2)}, u32[]{:S(2)}) collective-permute-start(bf16[1,128,3456]{2,1,0:T(8,128)(2,1)} %collective-permute-done.34), channel_id=1, source_target_pairs={{0,4},{4,0},{8,12},{12,8},{1,5},{5,1},{9,13},{13,9},{2,6},{6,2},{1... | collective-permute-start | bytes 2654216 | tf_op jit(solution)/shard_map/ppermute | solution.py:41
  346.7 55.7 %collective-permute-start.39 = (bf16[1,256,3456]{2,1,0:T(8,128)(2,1)}, bf16[1,256,3456]{2,1,0:T(8,128)(2,1)}, u32[]{:S(2)}, u32[]{:S(2)}) collective-permute-start(bf16[1,256,3456]{2,1,0:T(8,128)(2,1)} %get-tuple-element.81), channel_id=1, source_target_pairs={{0,4},{4,0},{8,12},{12,8},{1,5},{5,1},{9,13},{13,9},{2,6},{6,2},{1... | collective-permute-start | bytes 5308424 | tf_op jit(solution)/shard_map/ppermute | solution.py:41
  346.9 58.6 %collective-permute-start.38 = (bf16[1,256,3456]{2,1,0:T(8,128)(2,1)}, bf16[1,256,3456]{2,1,0:T(8,128)(2,1)}, u32[]{:S(2)}, u32[]{:S(2)}) collective-permute-start(bf16[1,256,3456]{2,1,0:T(8,128)(2,1)} %get-tuple-element.80), channel_id=1, source_target_pairs={{0,4},{4,0},{8,12},{12,8},{1,5},{5,1},{9,13},{13,9},{2,6},{6,2},{1... | collective-permute-start | bytes 5308424 | tf_op jit(solution)/shard_map/ppermute | solution.py:41
  350.8 242.0 %reduce-scatter.10.cloned.1.call-start = ((), (), s32[]{:S(2)}) async-start(), calls=%async_computation.9 | async-start | bytes 1310720 | tf_op jit(solution)/shard_map/reduce_scatter | solution.py:179
  411.7 53.1 %collective-permute-start.41 = (bf16[1,128,3456]{2,1,0:T(8,128)(2,1)}, bf16[1,128,3456]{2,1,0:T(8,128)(2,1)}, u32[]{:S(2)}, u32[]{:S(2)}) collective-permute-start(bf16[1,128,3456]{2,1,0:T(8,128)(2,1)} %collective-permute-done.40), channel_id=1, source_target_pairs={{0,4},{4,0},{8,12},{12,8},{1,5},{5,1},{9,13},{13,9},{2,6},{6,2},{1... | collective-permute-start | bytes 2654216 | tf_op jit(solution)/shard_map/ppermute | solution.py:41
  452.1 141.6 %reduce-scatter.14.cloned.1.call-start = ((), (), s32[]{:S(2)}) async-start(), calls=%async_computation.12 | async-start | bytes 1310720 | tf_op jit(solution)/shard_map/reduce_scatter | solution.py:179
  461.8 56.5 %collective-permute-start.55 = (bf16[1,128,3456]{2,1,0:T(8,128)(2,1)}, bf16[1,128,3456]{2,1,0:T(8,128)(2,1)}, u32[]{:S(2)}, u32[]{:S(2)}) collective-permute-start(bf16[1,128,3456]{2,1,0:T(8,128)(2,1)} %collective-permute-done.54), channel_id=1, source_target_pairs={{0,4},{4,0},{8,12},{12,8},{1,5},{5,1},{9,13},{13,9},{2,6},{6,2},{1... | collective-permute-start | bytes 2654216 | tf_op jit(solution)/shard_map/ppermute | solution.py:41
  470.2 124.6 %reduce-scatter.16.cloned.1.call-start = ((), (), s32[]{:S(2)}) async-start(), calls=%async_computation.13 | async-start | bytes 1310720 | tf_op jit(solution)/shard_map/reduce_scatter | solution.py:179
  538.7 57.0 %reduce-scatter.18.cloned.1.call-start = ((), (), s32[]{:S(2)}) async-start(), calls=%async_computation.14 | async-start | bytes 655360 | tf_op jit(solution)/shard_map/reduce_scatter | solution.py:179
  (119 other events, 2044.1 us)
Sparse Core Ops, SparseCore 0:
  9.6 100.7 all-gather.2
  112.6 19.9 reduce-scatter.11
  164.5 34.2 all-reduce.1
  350.9 24.4 reduce-scatter.7
  452.2 24.5 reduce-scatter.9
  479.1 25.8 reduce-scatter.13
  538.9 25.3 reduce-scatter.15
  566.6 20.1 reduce-scatter.17
  591.8 18.8 reduce-scatter.19
